TPU v7x, 256 devices: a whole 4x4x8 slice. The times are simulated.
256 devices in a mesh: loop: 4 (over y_hi, core), inner: 64 (over z, x, y_lo).
Axes of the slice: x: 4, y: 4 (y_hi: 2, y_lo: 2; y = y_hi * 2 + y_lo), z: 8, core: 2. Of those that a mesh axis runs over, the one named last changes fastest.
Arguments:
- snapshots: bfloat16 [65536, 1024], P(('loop', 'inner')), may hold values from -6 to 6
- bins: int32 [65536], replicated, may hold values from 0 to 511, as said below
- pairs: int32 [2048, 2], replicated, may hold values from 0 to 511, as said below
- start_weights: bfloat16 [1024, 32], replicated, may hold values from -0.1875 to 0.1875
Outputs:
- basis: float32 [65536, 96], P(('loop', 'inner'))
- coefficients: float32 [4, 32, 32], replicated
Inputs may be any that keep to these rules, and one draw needn't show every extreme that they name: `bins`: the snapshot in row n has a bin in [r * 8, (r + 1) * 8), where r = (n // 256) mod (64). `pairs`: every row (a, b) has a <= b <= a + 8; every bin is paired with itself.
All inputs are finite; a program needn't handle non-finite values.
Results may differ from a plain program's by a relative error of at most 0.0003.
Values may be sent and summed in bfloat16 or wider, within the bound.
A program may use at most 64 MiB of HBM per device.

v0:
```python
import jax
import jax.numpy as jnp
from jax import lax
from jax.sharding import PartitionSpec as P

STEPS = 2
BINS_COL = 8


def extended(cells, sides, width):
    for axis, dim in sides:
        count = lax.axis_size(axis)
        ends = count - 1
        head = lax.slice_in_dim(cells, 0, width, axis=dim)
        tail = lax.slice_in_dim(cells, cells.shape[dim] - width, cells.shape[dim], axis=dim)
        cells = jnp.concatenate(
            [
                lax.ppermute(tail, axis, [(i, (i + 1) % count) for i in range(ends)]),
                cells,
                lax.ppermute(head, axis, [((i + 1) % count, i) for i in range(ends)]),
            ],
            axis=dim,
        )
    return cells


def matches(values, targets):
    return (values[:, None] == targets[None, :]).astype(jnp.float32)


def local_gram(left, right):
    return jnp.dot(left.T, right, precision=lax.Precision.HIGHEST)


def finish(matrix, gram_total):
    lower_factor = jnp.linalg.cholesky(gram_total)
    result = lax.linalg.triangular_solve(
        lower_factor, matrix, left_side=False, lower=True, transpose_a=True
    )
    return (result, lower_factor.T)


def local(snapshots, bins, pairs, start_weights):
    row_count, features = snapshots.shape
    block_width = start_weights.shape[1]
    n_loop = lax.axis_size("loop")
    n_inner = lax.axis_size("inner")
    column = lax.axis_index("inner")
    group = lax.axis_index("loop")
    bin_grid = jnp.pad(
        bins.reshape(n_loop, n_inner, row_count), ((0, 0), (1, 1), (0, 0)), constant_values=-1
    )
    stacked = lax.all_gather(snapshots[None], "loop", axis=0, tiled=True)
    partner_rows = extended(stacked, (("inner", 1),), row_count)
    tile_rows = partner_rows.reshape(n_loop * 3 * row_count, features)
    tile_bins = lax.dynamic_slice_in_dim(bin_grid, column, 3, 1).reshape(-1)
    my_bins = lax.dynamic_slice_in_dim(bins, (group * n_inner + column) * row_count, row_count)
    bin_base = column * BINS_COL
    my_ids = bin_base + jnp.arange(BINS_COL, dtype=jnp.int32)
    window_ids = bin_base - BINS_COL + jnp.arange(3 * BINS_COL, dtype=jnp.int32)
    left_bins = pairs[:, 0]
    right_bins = pairs[:, 1]
    pair_count = jnp.dot(
        matches(left_bins, my_ids).T,
        matches(right_bins, window_ids),
        precision=lax.Precision.HIGHEST,
    )
    pair_count = pair_count + jnp.dot(
        matches(right_bins, my_ids).T,
        matches(left_bins, window_ids),
        precision=lax.Precision.HIGHEST,
    )
    linked_bins = jnp.where(pair_count > 0.5, 1.0, 0.0).astype(jnp.float32)
    my_hot = matches(my_bins, my_ids)
    row_links = jnp.dot(my_hot, linked_bins)
    mine_wide = snapshots.astype(jnp.float32)
    mine_norms = jnp.sum(mine_wide * mine_wide, axis=1)
    epsilon = features / 3.0
    part_hot = matches(tile_bins, window_ids) * (tile_bins >= 0).astype(jnp.float32)[:, None]
    band_mask = jnp.dot(row_links, part_hot.T)
    part_wide = tile_rows.astype(jnp.float32)
    part_norms = jnp.sum(part_wide * part_wide, axis=1)
    products = lax.dot_general(
        snapshots, tile_rows, (((1,), (1,)), ((), ())), preferred_element_type=jnp.float32
    )
    distance = mine_norms[:, None] + part_norms[None, :] - 2.0 * products
    kept_tiles = [band_mask * jnp.exp(-distance / epsilon)]

    def current_kernel(which):
        return kept_tiles[which]

    degree = jnp.sum(current_kernel(0), axis=1)
    inv_root = lax.rsqrt(degree)
    start_block = jnp.dot(snapshots, start_weights, preferred_element_type=jnp.float32)
    start_total = lax.psum(local_gram(start_block, start_block), ("loop", "inner"))
    current, unused = finish(start_block, start_total)
    basis_blocks = [current]
    coefficients = []
    previous = current
    prev_b = jnp.zeros((block_width, block_width), jnp.float32)
    for lanczos_step in range(STEPS):
        scaled = inv_root[:, None] * current
        vec_stack = lax.all_gather(scaled[None], "loop", axis=0, tiled=True)
        vec_strip = extended(vec_stack, (("inner", 1),), row_count)
        strip = vec_strip.reshape(n_loop * 3 * row_count, block_width)
        total = jnp.dot(current_kernel(0), strip, precision=lax.Precision.HIGHEST)
        image = inv_root[:, None] * total
        projected = lax.psum(local_gram(current, image), ("loop", "inner"))
        image = image - jnp.dot(current, projected, precision=lax.Precision.HIGHEST)
        if lanczos_step > 0:
            image = image - jnp.dot(previous, prev_b.T, precision=lax.Precision.HIGHEST)
        gram_total = lax.psum(local_gram(image, image), ("loop", "inner"))
        following, factor = finish(image, gram_total)
        coefficients.append(projected)
        coefficients.append(factor)
        previous = current
        prev_b = factor
        current = following
        basis_blocks.append(current)
    return (jnp.concatenate(basis_blocks, axis=1), jnp.stack(coefficients))


def solution(mesh):
    in_specs = (P(("loop", "inner"), None), P(), P(), P())
    out_specs = (P(("loop", "inner"), None), P())
    return jax.shard_map(local, mesh=mesh, in_specs=in_specs, out_specs=out_specs, check_vma=False)
```

profile of v0, /device:TPU:1, one launch (start us, length us, event | category | flops | bytes accessed | tf_op | source)
XLA Modules:
  0.0 579.3 jit_solution(10393950573843033094)
XLA Ops:
  9.8 1.3 fusion.49
  11.2 90.2 %psum.35 = f32[32,32]{0,1:T(8,128)S(1)} all-reduce(f32[32,32]{0,1:T(8,128)S(1)} %fusion.50), channel_id=1, replica_groups=mesh['loop'=4,'inner'=64] {'loop','inner'}, use_global_device_ids=true, to_apply=%region_0.1 | all-reduce | flops 1024 | bytes 8192 | tf_op jit(solution)/shard_map/psum | solution.py:95
  101.5 1.3 collective-permute-start.1
  102.8 5.3 collective-permute-start
  108.1 2.9 cholesky.59
  112.4 2.4 custom-call.7
  114.8 1.2 multiply_reduce_fusion.1
  118.8 31.0 %collective-permute-done.1 = bf16[4,256,1024]{2,1,0:T(8,128)(2,1)S(1)} collective-permute-done((bf16[4,256,1024]{2,1,0:T(8,128)(2,1)}, bf16[4,256,1024]{2,1,0:T(8,128)(2,1)S(1)}, u32[]{:S(2)}, u32[]{:S(2)}) %collective-permute-start.1) | collective-permute-done | bytes 2097184 | tf_op jit(solution)/shard_map/ppermute | solution.py:20
  149.8 44.7 %collective-permute-done = bf16[4,256,1024]{2,1,0:T(8,128)(2,1)} collective-permute-done((bf16[4,256,1024]{2,1,0:T(8,128)(2,1)}, bf16[4,256,1024]{2,1,0:T(8,128)(2,1)}, u32[]{:S(2)}, u32[]{:S(2)}) %collective-permute-start) | collective-permute-done | bytes 2097184 | tf_op jit(solution)/shard_map/ppermute | solution.py:18
  194.5 3.6 multiply_reduce_fusion
  198.2 3.5 fusion
  201.7 3.1 fusion.46
  205.0 7.2 %all-gather.1 = f32[1024,32]{0,1:T(8,128)S(1)} all-gather(f32[256,32]{0,1:T(8,128)S(1)} %get-tuple-element.20), channel_id=3, replica_groups=mesh['loop'=4,'inner'=64] {'loop'}, dimensions={0}, use_global_device_ids=true | all-gather | bytes 163840 | tf_op jit(solution)/shard_map/all_gather | solution.py:103
  212.3 1.3 collective-permute-start.3
  213.6 4.8 collective-permute-start.2
  218.4 1.9 collective-permute-done.3
  220.2 3.2 collective-permute-done.2
  223.6 2.8 convolution_multiply_fusion.3
  226.5 80.3 %psum.36 = f32[32,32]{0,1:T(8,128)S(1)} all-reduce(f32[32,32]{0,1:T(8,128)S(1)} %fusion.51), channel_id=1, replica_groups=mesh['loop'=4,'inner'=64] {'loop','inner'}, use_global_device_ids=true, to_apply=%region_6.9 | all-reduce | flops 1024 | bytes 8192 | tf_op jit(solution)/shard_map/psum | solution.py:108
  307.2 75.5 %psum.37 = f32[32,32]{0,1:T(8,128)S(1)} all-reduce(f32[32,32]{0,1:T(8,128)S(1)} %fusion.52), channel_id=1, replica_groups=mesh['loop'=4,'inner'=64] {'loop','inner'}, use_global_device_ids=true, to_apply=%region_7.10 | all-reduce | flops 1024 | bytes 8192 | tf_op jit(solution)/shard_map/psum | solution.py:112
  382.8 2.9 cholesky.70
  387.6 2.4 custom-call.8
  390.3 7.4 %all-gather.2 = f32[1024,32]{0,1:T(8,128)S(1)} all-gather(f32[256,32]{0,1:T(8,128)S(1)} %get-tuple-element.22), channel_id=4, replica_groups=mesh['loop'=4,'inner'=64] {'loop'}, dimensions={0}, use_global_device_ids=true | all-gather | bytes 163840 | tf_op jit(solution)/shard_map/all_gather | solution.py:103
  397.8 1.3 collective-permute-start.5
  399.1 4.0 collective-permute-start.4
  403.1 1.5 collective-permute-done.5
  404.7 2.6 collective-permute-done.4
  407.5 3.5 convolution_multiply_fusion.2
  411.1 76.5 %psum.38 = f32[32,32]{0,1:T(8,128)S(1)} all-reduce(f32[32,32]{0,1:T(8,128)S(1)} %fusion.53), channel_id=1, replica_groups=mesh['loop'=4,'inner'=64] {'loop','inner'}, use_global_device_ids=true, to_apply=%region_8.11 | all-reduce | flops 1024 | bytes 8192 | tf_op jit(solution)/shard_map/psum | solution.py:108
  488.7 75.3 %psum.39 = f32[32,32]{0,1:T(8,128)S(1)} all-reduce(f32[32,32]{0,1:T(8,128)S(1)} %fusion.54), channel_id=1, replica_groups=mesh['loop'=4,'inner'=64] {'loop','inner'}, use_global_device_ids=true, to_apply=%region_9.12 | all-reduce | flops 1024 | bytes 8192 | tf_op jit(solution)/shard_map/psum | solution.py:112
  564.1 2.9 cholesky.81
  568.4 2.4 custom-call.9
  (62 shorter events, 14.6 us)
Async XLA Ops:
  7.2 2.6 copy-start
  7.2 94.4 %all-gather.5.cloned.1.call-start = ((), (), s32[]{:S(2)}) async-start(), calls=%async_computation | async-start | bytes 2621440 | tf_op jit(solution)/shard_map/all_gather | solution.py:53
  101.5 48.3 %collective-permute-start.1 = (bf16[4,256,1024]{2,1,0:T(8,128)(2,1)}, bf16[4,256,1024]{2,1,0:T(8,128)(2,1)S(1)}, u32[]{:S(2)}, u32[]{:S(2)}) collective-permute-start(bf16[4,256,1024]{2,1,0:T(8,128)(2,1)} %bitcast.93), channel_id=1, source_target_pairs={{1,0},{2,1},{3,2},{4,3},{5,4},{6,5},{7,6},{8,7},{9,8},{10,9},{11,1... | collective-permute-start | bytes 6291464 | tf_op jit(solution)/shard_map/ppermute | solution.py:20
  102.8 91.7 %collective-permute-start = (bf16[4,256,1024]{2,1,0:T(8,128)(2,1)}, bf16[4,256,1024]{2,1,0:T(8,128)(2,1)}, u32[]{:S(2)}, u32[]{:S(2)}) collective-permute-start(bf16[4,256,1024]{2,1,0:T(8,128)(2,1)} %bitcast.94), channel_id=1, source_target_pairs={{0,1},{1,2},{2,3},{3,4},{4,5},{5,6},{6,7},{7,8},{8,9},{9,10},{10,1... | collective-permute-start | bytes 6291464 | tf_op jit(solution)/shard_map/ppermute | solution.py:18
  118.8 79.3 %copy-start.1 = (bf16[256,1024]{1,0:T(8,128)(2,1)S(1)}, bf16[256,1024]{1,0:T(8,128)(2,1)}, u32[]{:S(2)}) copy-start(bf16[256,1024]{1,0:T(8,128)(2,1)} %param.7) | copy-start | bytes 1572868
  204.8 185.5 %copy-start.5 = (f32[256]{0:T(256)}, f32[256]{0:T(256)S(1)}, u32[]{:S(2)}) copy-start(f32[256]{0:T(256)S(1)} %rsqrt.7) | copy-start | bytes 3076
  212.3 7.9 %collective-permute-start.3 = (f32[4,256,32]{1,0,2:T(4,128)S(1)}, f32[4,256,32]{1,0,2:T(4,128)S(1)}, u32[]{:S(2)}, u32[]{:S(2)}) collective-permute-start(f32[4,256,32]{1,0,2:T(4,128)S(1)} %reshape.60), channel_id=1, source_target_pairs={{1,0},{2,1},{3,2},{4,3},{5,4},{6,5},{7,6},{8,7},{9,8},{10,9},{11,1... | collective-permute-start | bytes 393224 | tf_op jit(solution)/shard_map/ppermute | solution.py:20
  213.6 9.8 %collective-permute-start.2 = (f32[4,256,32]{1,0,2:T(4,128)S(1)}, f32[4,256,32]{1,0,2:T(4,128)S(1)}, u32[]{:S(2)}, u32[]{:S(2)}) collective-permute-start(f32[4,256,32]{1,0,2:T(4,128)S(1)} %reshape.60), channel_id=1, source_target_pairs={{0,1},{1,2},{2,3},{3,4},{4,5},{5,6},{6,7},{7,8},{8,9},{9,10},{10,1... | collective-permute-start | bytes 393224 | tf_op jit(solution)/shard_map/ppermute | solution.py:18
  306.9 83.4 %copy-start.2 = (f32[32,32]{0,1:T(8,128)}, f32[32,32]{0,1:T(8,128)S(1)}, u32[]{:S(2)}) copy-start(f32[32,32]{0,1:T(8,128)S(1)} %psum.36) | copy-start | bytes 12292
  397.8 173.9 %copy-start.3 = (f32[32,32]{0,1:T(8,128)S(1)}, f32[32,32]{0,1:T(8,128)}, u32[]{:S(2)}) copy-start(f32[32,32]{0,1:T(8,128)} %copy-done.2) | copy-start | bytes 12292
  397.8 173.9 %copy-start.4 = (f32[1,32,32]{1,2,0:T(8,128)S(1)}, f32[1,32,32]{1,2,0:T(8,128)}, u32[]{:S(2)}) copy-start(f32[1,32,32]{1,2,0:T(8,128)} %get-tuple-element.12) | copy-start | bytes 12292
  397.8 6.8 %collective-permute-start.5 = (f32[4,256,32]{1,0,2:T(4,128)S(1)}, f32[4,256,32]{1,0,2:T(4,128)S(1)}, u32[]{:S(2)}, u32[]{:S(2)}) collective-permute-start(f32[4,256,32]{1,0,2:T(4,128)S(1)} %reshape.61), channel_id=1, source_target_pairs={{1,0},{2,1},{3,2},{4,3},{5,4},{6,5},{7,6},{8,7},{9,8},{10,9},{11,1... | collective-permute-start | bytes 393224 | tf_op jit(solution)/shard_map/ppermute | solution.py:20
  399.1 8.2 %collective-permute-start.4 = (f32[4,256,32]{1,0,2:T(4,128)S(1)}, f32[4,256,32]{1,0,2:T(4,128)S(1)}, u32[]{:S(2)}, u32[]{:S(2)}) collective-permute-start(f32[4,256,32]{1,0,2:T(4,128)S(1)} %reshape.61), channel_id=1, source_target_pairs={{0,1},{1,2},{2,3},{3,4},{4,5},{5,6},{6,7},{7,8},{8,9},{9,10},{10,1... | collective-permute-start | bytes 393224 | tf_op jit(solution)/shard_map/ppermute | solution.py:18
Sparse Core Ops, SparseCore 0:
  9.8 33.8 all-gather.4
where the time goes:
time: 581 us; the launch traced here: 579 us
  blocking collectives  413 us (71%)
  waiting for transfers between devices  85.5 us (15%)
  other arithmetic  26.3 us (5%)
  matrix products  18.7 us (3%)
  starting transfers between devices  17.9 us (3%)
  between operations  14.3 us (2%)
    psum x2, blocking collectives, local(): projected = lax.psum(local_gram(current, image), ('loop', 'inner'))  157 us
    psum x2, blocking collectives, local(): gram_total = lax.psum(local_gram(image, image), ('loop', 'inner'))  151 us
    psum x1, blocking collectives, local(): lax.psum(local_gram(start_block, start_block), ('loop', 'inner'))  90.2 us
    ppermute x3, waiting for transfers between devices, extended(): lax.ppermute(tail, axis, [(i, (i + 1) % count) for i in range(ends)])  50.5 us
    ppermute x3, waiting for transfers between devices, extended(): lax.ppermute(head, axis, [((i + 1) % count, i) for i in range(ends)])  34.4 us
    all_gather x2, blocking collectives, local(): vec_stack = lax.all_gather(scaled[None], 'loop', axis=0, tiled=True)  14.7 us
    ppermute x3, starting transfers between devices, extended(): lax.ppermute(tail, axis, [(i, (i + 1) % count) for i in range(ends)])  14 us
  transfers between devices with their start and end apart: 7, of which 6 were waited for; matrix products, arithmetic and copies ran while one was open for 2% of the time, Pallas kernels for 0%

commit v1 on v0

--- a/solution.py
+++ b/solution.py
@@ -92,7 +92,9 @@
     degree = jnp.sum(current_kernel(0), axis=1)
     inv_root = lax.rsqrt(degree)
     start_block = jnp.dot(snapshots, start_weights, preferred_element_type=jnp.float32)
-    start_total = lax.psum(local_gram(start_block, start_block), ("loop", "inner"))
+    start_total = jnp.sum(
+        lax.all_gather(local_gram(start_block, start_block), ("loop", "inner")), axis=0
+    )
     current, unused = finish(start_block, start_total)
     basis_blocks = [current]
     coefficients = []

time: 581 us -> 1170 us (2.01)
  waiting for transfers between devices: 85.5 us -> 758 us
  blocking collectives: 413 us -> 331 us
    all_gather x0 -> x1, waiting for transfers between devices: none -> 719 us  [local(): lax.all_gather(local_gram(start_block, start_block), ('loop', 'inner'))]
    psum x1 -> x0, blocking collectives: 90.2 us -> none  [local(): lax.psum(local_gram(start_block, start_block), ('loop', 'inner'))]
    ppermute x3, waiting for transfers between devices: 50.5 us -> 2.64 us  [extended(): lax.ppermute(tail, axis, [(i, (i + 1) % count) for i in range(ends)])]
    all_gather x1, waiting for transfers between devices: 0.01 us -> 32.1 us  [local(): stacked = lax.all_gather(snapshots[None], 'loop', axis=0, tiled=True)]
    ppermute x3, waiting for transfers between devices: 34.4 us -> 3.07 us  [extended(): lax.ppermute(head, axis, [((i + 1) % count, i) for i in range(ends)])]
  transfers between devices with their start and end apart: 7 -> 8, of which waited for: 6 -> 6; matrix products, arithmetic and copies ran while one was open for 2% -> 1% of each run, Pallas kernels for 0% -> 0%
where the time goes in v1:
time: 1170 us
  waiting for transfers between devices  758 us (65%)
  blocking collectives  331 us (28%)
  other arithmetic  28.9 us (2%)
  matrix products  19.3 us (2%)
  starting transfers between devices  17.4 us (1%)
  between operations  14.4 us (1%)
    all_gather x1, waiting for transfers between devices, local(): lax.all_gather(local_gram(start_block, start_block), ('loop', 'inner'))  719 us
    psum x2, blocking collectives, local(): projected = lax.psum(local_gram(current, image), ('loop', 'inner'))  167 us
    psum x2, blocking collectives, local(): gram_total = lax.psum(local_gram(image, image), ('loop', 'inner'))  149 us
    all_gather x1, waiting for transfers between devices, local(): stacked = lax.all_gather(snapshots[None], 'loop', axis=0, tiled=True)  32.1 us
  transfers between devices with their start and end apart: 8, of which 6 were waited for; matrix products, arithmetic and copies ran while one was open for 1% of the time, Pallas kernels for 0%

profile of v1, /device:TPU:1, one launch (start us, length us, event | category | flops | bytes accessed | tf_op | source)
XLA Modules:
  0.0 1172.5 jit_solution(9403220896869877110)
XLA Ops:
  8.0 1.3 fusion.49
  11.2 32.1 %all-gather.9.cloned.1.call-done = bf16[1024,1024]{1,0:T(8,128)(2,1)} async-done(((bf16[256,1024]{1,0:T(8,128)(2,1)}), bf16[1024,1024]{1,0:T(8,128)(2,1)}) %all-gather.9.cloned.1.call-update) | async-done | bytes 2097168 | tf_op jit(solution)/shard_map/all_gather | solution.py:53
  43.3 1.4 collective-permute-start.1
  44.7 5.4 collective-permute-start
  50.9 1.2 multiply_reduce_fusion.1
  54.9 719.2 %all-gather.7.cloned.1.call-done = f32[8192,32]{1,0:T(8,128)} async-done(((f32[32,32]{1,0:T(8,128)}), f32[8192,32]{1,0:T(8,128)}) %all-gather.7.cloned.1.call-update) | async-done | bytes 1048592 | tf_op jit(solution)/shard_map/all_gather | solution.py:96
  774.1 2.5 reduce_sum.36
  776.7 2.9 cholesky.59
  781.0 2.4 custom-call.7
  783.5 3.7 multiply_reduce_fusion
  787.2 3.5 fusion
  790.7 3.1 fusion.46
  794.0 7.8 all-gather.2
  801.9 1.3 collective-permute-start.3
  803.2 4.0 collective-permute-start.2
  807.2 1.5 collective-permute-done.3
  809.8 2.8 convolution_multiply_fusion.3
  812.7 89.1 %psum.28 = f32[32,32]{0,1:T(8,128)S(1)} all-reduce(f32[32,32]{0,1:T(8,128)S(1)} %fusion.51), channel_id=1, replica_groups=mesh['loop'=4,'inner'=64] {'loop','inner'}, use_global_device_ids=true, to_apply=%region_6.9 | all-reduce | flops 1024 | bytes 8192 | tf_op jit(solution)/shard_map/psum | solution.py:110
  902.2 73.4 %psum.29 = f32[32,32]{0,1:T(8,128)S(1)} all-reduce(f32[32,32]{0,1:T(8,128)S(1)} %fusion.52), channel_id=1, replica_groups=mesh['loop'=4,'inner'=64] {'loop','inner'}, use_global_device_ids=true, to_apply=%region_7.10 | all-reduce | flops 1024 | bytes 8192 | tf_op jit(solution)/shard_map/psum | solution.py:114
  975.7 2.9 cholesky.70
  979.3 1.2 fusion.38
  980.4 2.4 custom-call.8
  983.1 7.6 all-gather.3
  990.8 1.3 collective-permute-start.5
  992.1 4.0 collective-permute-start.4
  996.1 1.5 collective-permute-done.5
  997.7 1.8 collective-permute-done.4
  999.6 3.5 convolution_multiply_fusion.2
  1003.3 77.5 %psum.30 = f32[32,32]{0,1:T(8,128)S(1)} all-reduce(f32[32,32]{0,1:T(8,128)S(1)} %fusion.53), channel_id=1, replica_groups=mesh['loop'=4,'inner'=64] {'loop','inner'}, use_global_device_ids=true, to_apply=%region_8.11 | all-reduce | flops 1024 | bytes 8192 | tf_op jit(solution)/shard_map/psum | solution.py:110
  1081.9 75.4 %psum.31 = f32[32,32]{0,1:T(8,128)S(1)} all-reduce(f32[32,32]{0,1:T(8,128)S(1)} %fusion.54), channel_id=1, replica_groups=mesh['loop'=4,'inner'=64] {'loop','inner'}, use_global_device_ids=true, to_apply=%region_9.12 | all-reduce | flops 1024 | bytes 8192 | tf_op jit(solution)/shard_map/psum | solution.py:114
  1157.4 2.9 cholesky.81
  1161.6 2.4 custom-call.9
  (67 shorter events, 15.0 us)
Async XLA Ops:
  7.2 0.8 copy-start
  7.2 36.1 %all-gather.9.cloned.1.call-start = ((), (), s32[]{:S(2)}) async-start(), calls=%async_computation.1 | async-start | bytes 2621440 | tf_op jit(solution)/shard_map/all_gather | solution.py:53
  7.9 766.2 %all-gather.7.cloned.1.call-start = ((), (), s32[]{:S(2)}) async-start(), calls=%async_computation | async-start | bytes 4210688 | tf_op jit(solution)/shard_map/all_gather | solution.py:96
  43.3 740.2 %copy-start.2 = (bf16[1024,1024]{1,0:T(8,128)(2,1)S(1)}, bf16[1024,1024]{1,0:T(8,128)(2,1)}, u32[]{:S(2)}) copy-start(bf16[1024,1024]{1,0:T(8,128)(2,1)} %all-gather.9.cloned.1.call-done) | copy-start | bytes 6291460
  43.3 740.1 %collective-permute-start.1 = (bf16[4,256,1024]{2,1,0:T(8,128)(2,1)}, bf16[4,256,1024]{2,1,0:T(8,128)(2,1)}, u32[]{:S(2)}, u32[]{:S(2)}) collective-permute-start(bf16[4,256,1024]{2,1,0:T(8,128)(2,1)} %bitcast.95), channel_id=1, source_target_pairs={{1,0},{2,1},{3,2},{4,3},{5,4},{6,5},{7,6},{8,7},{9,8},{10,9},{11,1... | collective-permute-start | bytes 6291464 | tf_op jit(solution)/shard_map/ppermute | solution.py:20
  44.7 738.7 %collective-permute-start = (bf16[4,256,1024]{2,1,0:T(8,128)(2,1)}, bf16[4,256,1024]{2,1,0:T(8,128)(2,1)}, u32[]{:S(2)}, u32[]{:S(2)}) collective-permute-start(bf16[4,256,1024]{2,1,0:T(8,128)(2,1)} %bitcast.96), channel_id=1, source_target_pairs={{0,1},{1,2},{2,3},{3,4},{4,5},{5,6},{6,7},{7,8},{8,9},{9,10},{10,1... | collective-permute-start | bytes 6291464 | tf_op jit(solution)/shard_map/ppermute | solution.py:18
  783.4 3.8 copy-start.1
  793.8 189.4 %copy-start.6 = (f32[256]{0:T(256)}, f32[256]{0:T(256)S(1)}, u32[]{:S(2)}) copy-start(f32[256]{0:T(256)S(1)} %rsqrt.7) | copy-start | bytes 3076
  801.9 6.8 collective-permute-start.3
  803.2 6.4 collective-permute-start.2
  901.9 81.3 %copy-start.3 = (f32[32,32]{0,1:T(8,128)}, f32[32,32]{0,1:T(8,128)S(1)}, u32[]{:S(2)}) copy-start(f32[32,32]{0,1:T(8,128)S(1)} %psum.28) | copy-start | bytes 12292
  990.8 174.1 %copy-start.4 = (f32[32,32]{0,1:T(8,128)S(1)}, f32[32,32]{0,1:T(8,128)}, u32[]{:S(2)}) copy-start(f32[32,32]{0,1:T(8,128)} %copy-done.3) | copy-start | bytes 12292
  990.8 174.1 %copy-start.5 = (f32[1,32,32]{1,2,0:T(8,128)S(1)}, f32[1,32,32]{1,2,0:T(8,128)}, u32[]{:S(2)}) copy-start(f32[1,32,32]{1,2,0:T(8,128)} %get-tuple-element.14) | copy-start | bytes 12292
  990.8 6.8 collective-permute-start.5
  992.1 7.3 collective-permute-start.4
Sparse Core Ops, SparseCore 0:
  9.8 33.3 all-gather.8
  45.7 728.3 all-gather.6
